TPU v7x, 32 devices: a whole 2x2x4 slice. The times are simulated.
32 devices in a mesh: gx: 8 (over y, x, core), gy: 4 (over z).
Axes of the slice: x: 2, y: 2, z: 4, core: 2. Of those that a mesh axis runs over, the one named last changes fastest.
Arguments:
- density: float32 [16, 64, 128], P('gx', 'gy'), may hold values from 0.8 to 1.6
- momentum: float32 [3, 16, 64, 128], P(None, 'gx', 'gy'), may hold values from -0.4 to 0.4
- energy: float32 [16, 64, 128], P('gx', 'gy'), may hold values from 2 to 3
- forcing: float32 [5, 16, 64, 128], P(None, 'gx', 'gy'), may hold values from -6 to 6
- coupling: float32 [2, 5, 5], replicated, may hold values from 0.22 to 1.1
- inverse: float32 [5, 5], replicated, may hold values from 0.09 to 0.63
Outputs:
- state_new: float32 [5, 16, 64, 128], P(None, 'gx', 'gy')
All inputs are finite; a program needn't handle non-finite values.
Results may differ from a plain program's by a relative error of at most 0.0003.
Values sent between devices are 32-bit elements; how exact they have to be, the bound alone decides.
A program may use at most 64 MiB of HBM per device.

v0:
```python
import jax
import jax.numpy as jnp
from jax import lax
from jax.sharding import PartitionSpec as P

precision_high = lax.Precision.HIGHEST
beta_coupling = 0.25
dissipation = 0.05


def extended_2(cells, sides, width):
    for axis, dim in sides:
        count = lax.axis_size(axis)
        ends = count - 1
        head = lax.slice_in_dim(cells, 0, width, axis=dim)
        tail = lax.slice_in_dim(cells, cells.shape[dim] - width, cells.shape[dim], axis=dim)
        cells = jnp.concatenate(
            [
                lax.ppermute(tail, axis, [(i, (i + 1) % count) for i in range(ends)]),
                cells,
                lax.ppermute(head, axis, [((i + 1) % count, i) for i in range(ends)]),
            ],
            axis=dim,
        )
    return cells


def from_behind(block, axis, distance):
    devices = range(lax.axis_size(axis))
    route = [(i - distance, i) for i in devices if i - distance in devices]
    return lax.ppermute(block, axis, route)


def apply_block(matrix, field):
    return jnp.einsum("ab,b...->a...", matrix, field, precision=precision_high)


def fluxes(state):
    density_safe = jnp.where(state[0] > 0.1, state[0], 1.0)
    momentum = state[1:4]
    energy = state[4]
    pressure = 0.4 * (energy - 0.5 * jnp.sum(momentum * momentum, axis=0) / density_safe)
    results = []
    for direction in range(3):
        velocity = momentum[direction] / density_safe
        components = [momentum[direction]]
        for component in range(3):
            extra = pressure if component == direction else 0.0
            components.append(momentum[component] * velocity + extra)
        components.append((energy + pressure) * velocity)
        results.append(jnp.stack(components))
    return jnp.stack(results)


def offset_core(array, axis, offset):
    lead_dims = array.ndim - 3
    slicer = [slice(None)] * lead_dims + [slice(2, -2), slice(2, -2), slice(2, -2)]
    length = array.shape[lead_dims + axis]
    slicer[lead_dims + axis] = slice(2 + offset, length - 2 + offset)
    return array[tuple(slicer)]


def residual_rhs(ext_state, ext_flux, forcing):
    residual_sum = forcing
    for direction in range(3):
        flux_dir = ext_flux[direction]
        residual_sum = residual_sum - 0.5 * (
            offset_core(flux_dir, direction, 1) - offset_core(flux_dir, direction, -1)
        )
        fourth = (
            offset_core(ext_state, direction, -2)
            - 4.0 * offset_core(ext_state, direction, -1)
            + 6.0 * offset_core(ext_state, direction, 0)
            - 4.0 * offset_core(ext_state, direction, 1)
            + offset_core(ext_state, direction, 2)
        )
        residual_sum = residual_sum - dissipation * fourth
    return residual_sum


def jacobian_term(matrix, sign_flip, velocity, field):
    return beta_coupling * (apply_block(matrix, field) + sign_flip * velocity * field)


def sweep(
    lead_term, cell_scale, vel_x, vel_y, mat_x, mat_y, sign_flip, west_face, south_face, inverse
):
    extent_x = lead_term.shape[1]
    extent_y = lead_term.shape[2]
    row_ids = jnp.arange(extent_x, dtype=jnp.int32)
    col_ids = jnp.arange(extent_y, dtype=jnp.int32)

    def step(state_carry, diag_num):
        prev_x, prev_y = state_carry
        columns = diag_num - row_ids
        is_valid = (columns >= 0) & (columns < extent_y)
        col_clip = jnp.clip(columns, 0, extent_y - 1)
        west_edge = lax.dynamic_index_in_dim(
            west_face, jnp.clip(diag_num, 0, extent_y - 1), axis=1, keepdims=True
        )
        from_west = jnp.concatenate([west_edge, prev_x[:, :-1]], axis=1)
        from_south = jnp.where((columns == 0)[None, :, None], south_face, prev_y)
        cell_lead = lead_term[:, row_ids, col_clip]
        scale_cells = cell_scale[row_ids, col_clip]
        fresh_cells = cell_lead - apply_block(inverse, from_west + from_south) / scale_cells
        fresh_cells = jnp.where(is_valid[None, :, None], fresh_cells, 0.0)
        jac_x = jacobian_term(mat_x, sign_flip, vel_x[row_ids, col_clip], fresh_cells)
        jac_y = jacobian_term(mat_y, sign_flip, vel_y[row_ids, col_clip], fresh_cells)
        return ((jac_x, jac_y), fresh_cells)

    initial = jnp.zeros((lead_term.shape[0], extent_x, lead_term.shape[3]), lead_term.dtype)
    diag_ids = jnp.arange(extent_x + extent_y - 1, dtype=jnp.int32)
    _, diagonals = lax.scan(step, (initial, initial), diag_ids)
    whole_block = diagonals[row_ids[:, None] + col_ids[None, :], :, row_ids[:, None], :]
    return jnp.transpose(whole_block, (2, 0, 1, 3))


def flip_field(array):
    return jnp.flip(array, axis=(array.ndim - 3, array.ndim - 2))


def wavefront(
    lead_term,
    cell_scale,
    vel_x,
    vel_y,
    mat_x,
    mat_y,
    sign_flip,
    inverse,
    chain_pos,
    blocks,
    send_x,
    send_y,
):
    nvars, extent_x, extent_y, extent_z = lead_term.shape
    block_depth = extent_z // blocks
    sections = blocks + lax.axis_size("gx") + lax.axis_size("gy") - 2

    def section(section_num, state_carry):
        whole_block, west_face, south_face = state_carry
        block_num = section_num - chain_pos
        is_active = (block_num >= 0) & (block_num < blocks)

        def work(current):
            solved = sweep(
                lead_term,
                cell_scale,
                vel_x,
                vel_y,
                mat_x,
                mat_y,
                sign_flip,
                west_face,
                south_face,
                inverse,
            )
            east_out = jacobian_term(mat_x, sign_flip, vel_x[-1], solved[:, -1])
            north_out = jacobian_term(mat_y, sign_flip, vel_y[:, -1], solved[:, :, -1])
            return (solved, east_out, north_out)

        def skip(current):
            return (
                current,
                jnp.zeros((nvars, extent_y, block_depth), jnp.float32),
                jnp.zeros((nvars, extent_x, block_depth), jnp.float32),
            )

        whole_block, east_out, north_out = lax.cond(is_active, work, skip, whole_block)
        return (whole_block, send_x(east_out), send_y(north_out))

    initial = (
        jnp.zeros_like(lead_term),
        jnp.zeros((nvars, extent_y, block_depth), jnp.float32),
        jnp.zeros((nvars, extent_x, block_depth), jnp.float32),
    )
    whole_block, _, _ = lax.fori_loop(0, sections, section, initial)
    return whole_block


def shards(density, momentum, energy, forcing, coupling, inverse):
    state = jnp.concatenate([density[None], momentum, energy[None]], axis=0)
    nvars = state.shape[0]
    z_pad = ((0, 0), (0, 0), (0, 0), (2, 2))
    own_flux = fluxes(state)
    stacked = jnp.concatenate([state, own_flux.reshape((3 * nvars,) + state.shape[1:])], axis=0)
    extended = extended_2(stacked, (("gx", 1), ("gy", 2)), 2)
    extended = jnp.pad(extended, z_pad)
    ext_state = extended[:nvars]
    ext_flux = extended[nvars:].reshape((3, nvars) + extended.shape[1:])
    rsd = residual_rhs(ext_state, ext_flux, forcing)
    vel_x = momentum[0] / density
    vel_y = momentum[1] / density
    vel_z = momentum[2] / density
    cell_scale = 1.0 + vel_x * vel_x + vel_y * vel_y + vel_z * vel_z
    lead_term = apply_block(inverse, rsd) / cell_scale
    blocks = 1
    pos_x = lax.axis_index("gx")
    pos_y = lax.axis_index("gy")
    lower_pos = pos_x + pos_y
    upper_pos = lax.axis_size("gx") - 1 - pos_x + (lax.axis_size("gy") - 1 - pos_y)

    def lower_send_x(face):
        return from_behind(face, "gx", 1)

    def lower_send_y(face):
        return from_behind(face, "gy", 1)

    def upper_send_x(face):
        return from_behind(face, "gx", -1)

    def upper_send_y(face):
        return from_behind(face, "gy", -1)

    lower = wavefront(
        lead_term,
        cell_scale,
        vel_x,
        vel_y,
        coupling[0],
        coupling[1],
        1.0,
        inverse,
        lower_pos,
        blocks,
        lower_send_x,
        lower_send_y,
    )
    upper = wavefront(
        flip_field(lower),
        flip_field(cell_scale),
        flip_field(vel_x),
        flip_field(vel_y),
        coupling[0].T,
        coupling[1].T,
        -1.0,
        inverse,
        upper_pos,
        blocks,
        upper_send_x,
        upper_send_y,
    )
    return state + flip_field(upper)


def solution(mesh):
    placed = (
        P("gx", "gy", None),
        P(None, "gx", "gy", None),
        P("gx", "gy", None),
        P(None, "gx", "gy", None),
        P(),
        P(),
    )
    return jax.shard_map(
        shards, mesh=mesh, in_specs=placed, out_specs=P(None, "gx", "gy", None), check_vma=False
    )
```

profile of v0, /device:TPU:0, one launch (start us, length us, event | category | flops | bytes accessed | tf_op | source)
XLA Modules:
  0.0 2131.9 jit_solution(17448762801251876829)
XLA Ops:
  8.2 3.1 collective-permute-start.5
  12.6 1.4 collective-permute-start.6
  14.0 5.6 collective-permute-start.7
  20.6 1.5 collective-permute-done.7
  24.0 771.4 %while.72 = (s32[]{:T(128)}, f32[5,2,16,128]{3,0,2,1:T(8,128)}, f32[5,16,128]{2,0,1:T(8,128)S(1)}, f32[5,2,128]{2,0,1:T(8,128)S(1)}, s32[]{:T(128)}, /*index=5*/...) while((s32[]{:T(128)}, f32[5,2,16,128]{3,0,2,1:T(8,128)}, ...), condition=%wide.region_6.7_spmd, body=%wide.region_1.6_spmd.sunk | while | flops 973770 | bytes 626535 | solution.py:177
  24.0 88.8 %conditional.4 = (f32[5,2,16,128]{3,0,2,1:T(8,128)}, f32[5,16,128]{2,0,1:T(8,128)S(1)}, f32[5,2,128]{2,0,1:T(8,128)S(1)}) conditional(s32[]{:T(128)} %convert_element_type.18, f32[5,2,16,128]{3,0,2,1:T(8,128)} %get-tuple-element.1465, (f32[5,2,16,128]{3,0,2,1:T(8,128)S(1)}, f32[5,16,128]{2,0,1:T(8,128)S(1)}, f32[5,2,128]{2,0,1:T(8,128)S(1)}, ...), branch_computations={%region_2.2_spmd, %region_3.5_spmd} | conditional | flops 973763 | bytes 441892 | solution.py:169
  24.0 85.4 %while.70 = (s32[]{:T(128)}, f32[5,2,128]{2,0,1:T(8,128)S(1)}, f32[5,2,128]{2,0,1:T(8,128)S(1)}, f32[17,5,2,128]{3,1,2,0:T(8,128)S(1)}, s32[17]{0:T(128)S(1)}, /...) while((s32[]{:T(128)}, f32[5,2,128]{2,0,1:T(8,128)S(1)}, ...), condition=%wide.region_5.4_spmd.clone.clone, body=%wide.region_4.3_spmd.clone.clone.sunk | while | flops 247715 | bytes 104944 | solution.py:113
  115.4 1.3 collective-permute-done.3
  116.8 89.2 %collective-permute-start.2 = (f32[5,16,128]{2,0,1:T(8,128)S(1)}, f32[5,16,128]{2,0,1:T(8,128)S(1)}, u32[]{:S(2)}, u32[]{:S(2)}) collective-permute-start(f32[5,16,128]{2,0,1:T(8,128)S(1)} %get-tuple-element.1279), channel_id=1, source_target_pairs={{0,4},{4,8},{8,12},{12,16},{16,20},{20,24},{24,28},{1,5},{5,9},{9,... | collective-permute-start | bytes 122888 | tf_op jit(solution)/shard_map/while/body/eval_jaxpr/ppermute | solution.py:31
  206.0 5.0 collective-permute-start.3
  211.1 1.3 collective-permute-done.3
  213.7 89.2 %collective-permute-start.3 = (f32[5,2,128]{2,0,1:T(8,128)S(1)}, f32[5,2,128]{2,0,1:T(8,128)S(1)}, u32[]{:S(2)}, u32[]{:S(2)}) collective-permute-start(f32[5,2,128]{2,0,1:T(8,128)S(1)} %get-tuple-element.1280), channel_id=1, source_target_pairs={{0,1},{1,2},{2,3},{4,5},{5,6},{6,7},{8,9},{9,10},{10,11},{12,13},{... | collective-permute-start | bytes 15368 | tf_op jit(solution)/shard_map/while/body/eval_jaxpr/ppermute | solution.py:31
  303.0 1.3 collective-permute-done.3
  305.7 5.6 collective-permute-start.3
  311.3 1.3 collective-permute-done.3
  312.7 87.7 %collective-permute-start.2 = (f32[5,16,128]{2,0,1:T(8,128)S(1)}, f32[5,16,128]{2,0,1:T(8,128)S(1)}, u32[]{:S(2)}, u32[]{:S(2)}) collective-permute-start(f32[5,16,128]{2,0,1:T(8,128)S(1)} %get-tuple-element.1279), channel_id=1, source_target_pairs={{0,4},{4,8},{8,12},{12,16},{16,20},{20,24},{24,28},{1,5},{5,9},{9,... | collective-permute-start | bytes 122888 | tf_op jit(solution)/shard_map/while/body/eval_jaxpr/ppermute | solution.py:31
  400.4 3.9 collective-permute-start.3
  404.4 1.3 collective-permute-done.3
  405.7 2.2 collective-permute-start.2
  408.0 90.7 %collective-permute-start.3 = (f32[5,2,128]{2,0,1:T(8,128)S(1)}, f32[5,2,128]{2,0,1:T(8,128)S(1)}, u32[]{:S(2)}, u32[]{:S(2)}) collective-permute-start(f32[5,2,128]{2,0,1:T(8,128)S(1)} %get-tuple-element.1280), channel_id=1, source_target_pairs={{0,1},{1,2},{2,3},{4,5},{5,6},{6,7},{8,9},{9,10},{10,11},{12,13},{... | collective-permute-start | bytes 15368 | tf_op jit(solution)/shard_map/while/body/eval_jaxpr/ppermute | solution.py:31
  498.6 1.3 collective-permute-done.3
  500.0 1.9 collective-permute-start.2
  502.0 4.2 collective-permute-start.3
  506.2 1.3 collective-permute-done.3
  507.5 86.3 %collective-permute-start.2 = (f32[5,16,128]{2,0,1:T(8,128)S(1)}, f32[5,16,128]{2,0,1:T(8,128)S(1)}, u32[]{:S(2)}, u32[]{:S(2)}) collective-permute-start(f32[5,16,128]{2,0,1:T(8,128)S(1)} %get-tuple-element.1279), channel_id=1, source_target_pairs={{0,4},{4,8},{8,12},{12,16},{16,20},{20,24},{24,28},{1,5},{5,9},{9,... | collective-permute-start | bytes 122888 | tf_op jit(solution)/shard_map/while/body/eval_jaxpr/ppermute | solution.py:31
  593.9 6.3 collective-permute-start.3
  600.2 1.3 collective-permute-done.3
  601.5 1.9 collective-permute-start.2
  603.5 88.6 %collective-permute-start.3 = (f32[5,2,128]{2,0,1:T(8,128)S(1)}, f32[5,2,128]{2,0,1:T(8,128)S(1)}, u32[]{:S(2)}, u32[]{:S(2)}) collective-permute-start(f32[5,2,128]{2,0,1:T(8,128)S(1)} %get-tuple-element.1280), channel_id=1, source_target_pairs={{0,1},{1,2},{2,3},{4,5},{5,6},{6,7},{8,9},{9,10},{10,11},{12,13},{... | collective-permute-start | bytes 15368 | tf_op jit(solution)/shard_map/while/body/eval_jaxpr/ppermute | solution.py:31
  693.5 2.3 collective-permute-start.2
  695.8 3.9 collective-permute-start.3
  701.1 88.7 %collective-permute-start.2 = (f32[5,16,128]{2,0,1:T(8,128)S(1)}, f32[5,16,128]{2,0,1:T(8,128)S(1)}, u32[]{:S(2)}, u32[]{:S(2)}) collective-permute-start(f32[5,16,128]{2,0,1:T(8,128)S(1)} %get-tuple-element.1279), channel_id=1, source_target_pairs={{0,4},{4,8},{8,12},{12,16},{16,20},{20,24},{24,28},{1,5},{5,9},{9,... | collective-permute-start | bytes 122888 | tf_op jit(solution)/shard_map/while/body/eval_jaxpr/ppermute | solution.py:31
  789.8 4.2 collective-permute-start.3
  796.9 1333.3 %while.73 = (s32[]{:T(128)}, f32[5,2,16,128]{3,0,2,1:T(8,128)}, f32[5,16,128]{2,0,1:T(8,128)S(1)}, f32[5,2,128]{2,0,1:T(8,128)S(1)}, s32[]{:T(128)}, /*index=5*/...) while((s32[]{:T(128)}, f32[5,2,16,128]{3,0,2,1:T(8,128)}, ...), condition=%wide.region_12.13_spmd, body=%wide.region_7.12_spmd.sunk | while | flops 976586 | bytes 630631 | solution.py:177
  799.6 4.5 collective-permute-done.1
  806.8 4.2 collective-permute-done.1
  811.0 77.8 %collective-permute-done = f32[5,16,128]{2,0,1:T(8,128)S(1)} collective-permute-done((f32[5,16,128]{2,0,1:T(8,128)S(1)}, f32[5,16,128]{2,0,1:T(8,128)S(1)}, u32[]{:S(2)}, u32[]{:S(2)}) %collective-permute-start) | collective-permute-done | bytes 40992 | tf_op jit(solution)/shard_map/while/body/eval_jaxpr/ppermute | solution.py:31
  891.5 4.5 collective-permute-done.1
  899.2 4.5 collective-permute-done.1
  907.0 82.4 %collective-permute-done.1 = f32[5,2,128]{2,0,1:T(8,128)S(1)} collective-permute-done((f32[5,2,128]{2,0,1:T(8,128)S(1)}, f32[5,2,128]{2,0,1:T(8,128)S(1)}, u32[]{:S(2)}, u32[]{:S(2)}) %collective-permute-start.1) | collective-permute-done | bytes 5152 | tf_op jit(solution)/shard_map/while/body/eval_jaxpr/ppermute | solution.py:31
  992.7 4.5 collective-permute-done.1
  1000.4 4.2 collective-permute-done.1
  1008.0 81.1 %collective-permute-done.1 = f32[5,2,128]{2,0,1:T(8,128)S(1)} collective-permute-done((f32[5,2,128]{2,0,1:T(8,128)S(1)}, f32[5,2,128]{2,0,1:T(8,128)S(1)}, u32[]{:S(2)}, u32[]{:S(2)}) %collective-permute-start.1) | collective-permute-done | bytes 5152 | tf_op jit(solution)/shard_map/while/body/eval_jaxpr/ppermute | solution.py:31
  1092.3 4.2 collective-permute-done.1
  1099.8 929.6 %collective-permute-done.1 = f32[5,2,128]{2,0,1:T(8,128)S(1)} collective-permute-done((f32[5,2,128]{2,0,1:T(8,128)S(1)}, f32[5,2,128]{2,0,1:T(8,128)S(1)}, u32[]{:S(2)}, u32[]{:S(2)}) %collective-permute-start.1) | collective-permute-done | bytes 5152 | tf_op jit(solution)/shard_map/while/body/eval_jaxpr/ppermute | solution.py:31
  2030.1 93.3 %conditional.5 = (f32[5,2,16,128]{3,0,2,1:T(8,128)}, f32[5,16,128]{2,0,1:T(8,128)S(1)}, f32[5,2,128]{2,0,1:T(8,128)S(1)}) conditional(s32[]{:T(128)} %convert_element_type.19, f32[5,2,16,128]{3,0,2,1:T(8,128)} %get-tuple-element.1507, (f32[5,2,16,128]{3,0,2,1:T(8,128)S(1)}, f32[5,16,128]{2,0,1:T(8,128)S(1)}, f32[5,2,128]{2,0,1:T(8,128)S(1)}, ...), branch_computations={%region_8.8_spmd, %region_9.11_spmd} | conditional | flops 976579 | bytes 445988 | solution.py:169
  2030.1 89.9 %while.71 = (s32[]{:T(128)}, f32[5,2,128]{2,0,1:T(8,128)S(1)}, f32[5,2,128]{2,0,1:T(8,128)S(1)}, f32[17,5,2,128]{3,1,2,0:T(8,128)S(1)}, s32[17]{0:T(128)S(1)}, /...) while((s32[]{:T(128)}, f32[5,2,128]{2,0,1:T(8,128)S(1)}, ...), condition=%wide.region_11.10_spmd.clone.clone, body=%wide.region_10.9_spmd.clone.clone.sunk | while | flops 248227 | bytes 109040 | solution.py:113
  2126.0 4.2 collective-permute-done.1
  (588 shorter events, 219.3 us)
Async XLA Ops:
  6.9 4.7 collective-permute-start.4
  8.2 4.3 collective-permute-start.5
  12.6 7.9 collective-permute-start.6
  14.0 8.0 collective-permute-start.7
  112.8 4.0 collective-permute-start.2
  114.1 2.6 collective-permute-start.3
  116.8 95.6 %collective-permute-start.2 = (f32[5,16,128]{2,0,1:T(8,128)S(1)}, f32[5,16,128]{2,0,1:T(8,128)S(1)}, u32[]{:S(2)}, u32[]{:S(2)}) collective-permute-start(f32[5,16,128]{2,0,1:T(8,128)S(1)} %get-tuple-element.1279), channel_id=1, source_target_pairs={{0,4},{4,8},{8,12},{12,16},{16,20},{20,24},{24,28},{1,5},{5,9},{9,... | collective-permute-start | bytes 122888 | tf_op jit(solution)/shard_map/while/body/eval_jaxpr/ppermute | solution.py:31
  206.0 6.4 collective-permute-start.3
  212.4 91.9 %collective-permute-start.2 = (f32[5,16,128]{2,0,1:T(8,128)S(1)}, f32[5,16,128]{2,0,1:T(8,128)S(1)}, u32[]{:S(2)}, u32[]{:S(2)}) collective-permute-start(f32[5,16,128]{2,0,1:T(8,128)S(1)} %get-tuple-element.1279), channel_id=1, source_target_pairs={{0,4},{4,8},{8,12},{12,16},{16,20},{20,24},{24,28},{1,5},{5,9},{9,... | collective-permute-start | bytes 122888 | tf_op jit(solution)/shard_map/while/body/eval_jaxpr/ppermute | solution.py:31
  213.7 90.6 %collective-permute-start.3 = (f32[5,2,128]{2,0,1:T(8,128)S(1)}, f32[5,2,128]{2,0,1:T(8,128)S(1)}, u32[]{:S(2)}, u32[]{:S(2)}) collective-permute-start(f32[5,2,128]{2,0,1:T(8,128)S(1)} %get-tuple-element.1280), channel_id=1, source_target_pairs={{0,1},{1,2},{2,3},{4,5},{5,6},{6,7},{8,9},{9,10},{10,11},{12,13},{... | collective-permute-start | bytes 15368 | tf_op jit(solution)/shard_map/while/body/eval_jaxpr/ppermute | solution.py:31
  304.4 8.3 collective-permute-start.2
  305.7 7.0 collective-permute-start.3
  312.7 93.0 %collective-permute-start.2 = (f32[5,16,128]{2,0,1:T(8,128)S(1)}, f32[5,16,128]{2,0,1:T(8,128)S(1)}, u32[]{:S(2)}, u32[]{:S(2)}) collective-permute-start(f32[5,16,128]{2,0,1:T(8,128)S(1)} %get-tuple-element.1279), channel_id=1, source_target_pairs={{0,4},{4,8},{8,12},{12,16},{16,20},{20,24},{24,28},{1,5},{5,9},{9,... | collective-permute-start | bytes 122888 | tf_op jit(solution)/shard_map/while/body/eval_jaxpr/ppermute | solution.py:31
  400.4 5.2 collective-permute-start.3
  405.7 94.3 %collective-permute-start.2 = (f32[5,16,128]{2,0,1:T(8,128)S(1)}, f32[5,16,128]{2,0,1:T(8,128)S(1)}, u32[]{:S(2)}, u32[]{:S(2)}) collective-permute-start(f32[5,16,128]{2,0,1:T(8,128)S(1)} %get-tuple-element.1279), channel_id=1, source_target_pairs={{0,4},{4,8},{8,12},{12,16},{16,20},{20,24},{24,28},{1,5},{5,9},{9,... | collective-permute-start | bytes 122888 | tf_op jit(solution)/shard_map/while/body/eval_jaxpr/ppermute | solution.py:31
  408.0 92.0 %collective-permute-start.3 = (f32[5,2,128]{2,0,1:T(8,128)S(1)}, f32[5,2,128]{2,0,1:T(8,128)S(1)}, u32[]{:S(2)}, u32[]{:S(2)}) collective-permute-start(f32[5,2,128]{2,0,1:T(8,128)S(1)} %get-tuple-element.1280), channel_id=1, source_target_pairs={{0,1},{1,2},{2,3},{4,5},{5,6},{6,7},{8,9},{9,10},{10,11},{12,13},{... | collective-permute-start | bytes 15368 | tf_op jit(solution)/shard_map/while/body/eval_jaxpr/ppermute | solution.py:31
  500.0 7.5 collective-permute-start.2
  502.0 5.5 collective-permute-start.3
  507.5 94.0 %collective-permute-start.2 = (f32[5,16,128]{2,0,1:T(8,128)S(1)}, f32[5,16,128]{2,0,1:T(8,128)S(1)}, u32[]{:S(2)}, u32[]{:S(2)}) collective-permute-start(f32[5,16,128]{2,0,1:T(8,128)S(1)} %get-tuple-element.1279), channel_id=1, source_target_pairs={{0,4},{4,8},{8,12},{12,16},{16,20},{20,24},{24,28},{1,5},{5,9},{9,... | collective-permute-start | bytes 122888 | tf_op jit(solution)/shard_map/while/body/eval_jaxpr/ppermute | solution.py:31
  593.9 7.6 collective-permute-start.3
  601.5 91.9 %collective-permute-start.2 = (f32[5,16,128]{2,0,1:T(8,128)S(1)}, f32[5,16,128]{2,0,1:T(8,128)S(1)}, u32[]{:S(2)}, u32[]{:S(2)}) collective-permute-start(f32[5,16,128]{2,0,1:T(8,128)S(1)} %get-tuple-element.1279), channel_id=1, source_target_pairs={{0,4},{4,8},{8,12},{12,16},{16,20},{20,24},{24,28},{1,5},{5,9},{9,... | collective-permute-start | bytes 122888 | tf_op jit(solution)/shard_map/while/body/eval_jaxpr/ppermute | solution.py:31
  603.5 90.0 %collective-permute-start.3 = (f32[5,2,128]{2,0,1:T(8,128)S(1)}, f32[5,2,128]{2,0,1:T(8,128)S(1)}, u32[]{:S(2)}, u32[]{:S(2)}) collective-permute-start(f32[5,2,128]{2,0,1:T(8,128)S(1)} %get-tuple-element.1280), channel_id=1, source_target_pairs={{0,1},{1,2},{2,3},{4,5},{5,6},{6,7},{8,9},{9,10},{10,11},{12,13},{... | collective-permute-start | bytes 15368 | tf_op jit(solution)/shard_map/while/body/eval_jaxpr/ppermute | solution.py:31
  693.5 7.6 collective-permute-start.2
  695.8 5.2 collective-permute-start.3
  701.1 94.3 %collective-permute-start.2 = (f32[5,16,128]{2,0,1:T(8,128)S(1)}, f32[5,16,128]{2,0,1:T(8,128)S(1)}, u32[]{:S(2)}, u32[]{:S(2)}) collective-permute-start(f32[5,16,128]{2,0,1:T(8,128)S(1)} %get-tuple-element.1279), channel_id=1, source_target_pairs={{0,4},{4,8},{8,12},{12,16},{16,20},{20,24},{24,28},{1,5},{5,9},{9,... | collective-permute-start | bytes 122888 | tf_op jit(solution)/shard_map/while/body/eval_jaxpr/ppermute | solution.py:31
  789.8 5.5 collective-permute-start.3
  797.0 7.1 collective-permute-start
  798.3 5.8 collective-permute-start.1
  804.2 84.7 %collective-permute-start = (f32[5,16,128]{2,0,1:T(8,128)S(1)}, f32[5,16,128]{2,0,1:T(8,128)S(1)}, u32[]{:S(2)}, u32[]{:S(2)}) collective-permute-start(f32[5,16,128]{2,0,1:T(8,128)S(1)} %get-tuple-element.1294), channel_id=1, source_target_pairs={{4,0},{8,4},{12,8},{16,12},{20,16},{24,20},{28,24},{5,1},{9,5},{13... | collective-permute-start | bytes 122888 | tf_op jit(solution)/shard_map/while/body/eval_jaxpr/ppermute | solution.py:31
  805.5 5.5 collective-permute-start.1
  888.9 7.8 collective-permute-start
  890.2 5.8 collective-permute-start.1
  896.6 7.8 collective-permute-start
  897.9 5.8 collective-permute-start.1
  904.4 85.6 %collective-permute-start = (f32[5,16,128]{2,0,1:T(8,128)S(1)}, f32[5,16,128]{2,0,1:T(8,128)S(1)}, u32[]{:S(2)}, u32[]{:S(2)}) collective-permute-start(f32[5,16,128]{2,0,1:T(8,128)S(1)} %get-tuple-element.1294), channel_id=1, source_target_pairs={{4,0},{8,4},{12,8},{16,12},{20,16},{24,20},{28,24},{5,1},{9,5},{13... | collective-permute-start | bytes 122888 | tf_op jit(solution)/shard_map/while/body/eval_jaxpr/ppermute | solution.py:31
  905.7 83.7 %collective-permute-start.1 = (f32[5,2,128]{2,0,1:T(8,128)S(1)}, f32[5,2,128]{2,0,1:T(8,128)S(1)}, u32[]{:S(2)}, u32[]{:S(2)}) collective-permute-start(f32[5,2,128]{2,0,1:T(8,128)S(1)} %get-tuple-element.1295), channel_id=1, source_target_pairs={{1,0},{2,1},{3,2},{5,4},{6,5},{7,6},{9,8},{10,9},{11,10},{13,12},{... | collective-permute-start | bytes 15368 | tf_op jit(solution)/shard_map/while/body/eval_jaxpr/ppermute | solution.py:31
  990.1 7.8 collective-permute-start
  991.4 5.8 collective-permute-start.1
  997.8 7.5 collective-permute-start
  999.1 5.5 collective-permute-start.1
  1005.4 84.3 %collective-permute-start = (f32[5,16,128]{2,0,1:T(8,128)S(1)}, f32[5,16,128]{2,0,1:T(8,128)S(1)}, u32[]{:S(2)}, u32[]{:S(2)}) collective-permute-start(f32[5,16,128]{2,0,1:T(8,128)S(1)} %get-tuple-element.1294), channel_id=1, source_target_pairs={{4,0},{8,4},{12,8},{16,12},{20,16},{24,20},{28,24},{5,1},{9,5},{13... | collective-permute-start | bytes 122888 | tf_op jit(solution)/shard_map/while/body/eval_jaxpr/ppermute | solution.py:31
  1006.7 82.4 %collective-permute-start.1 = (f32[5,2,128]{2,0,1:T(8,128)S(1)}, f32[5,2,128]{2,0,1:T(8,128)S(1)}, u32[]{:S(2)}, u32[]{:S(2)}) collective-permute-start(f32[5,2,128]{2,0,1:T(8,128)S(1)} %get-tuple-element.1295), channel_id=1, source_target_pairs={{1,0},{2,1},{3,2},{5,4},{6,5},{7,6},{9,8},{10,9},{11,10},{13,12},{... | collective-permute-start | bytes 15368 | tf_op jit(solution)/shard_map/while/body/eval_jaxpr/ppermute | solution.py:31
  1089.7 7.5 collective-permute-start
  1091.0 5.5 collective-permute-start.1
  1097.2 932.9 %collective-permute-start = (f32[5,16,128]{2,0,1:T(8,128)S(1)}, f32[5,16,128]{2,0,1:T(8,128)S(1)}, u32[]{:S(2)}, u32[]{:S(2)}) collective-permute-start(f32[5,16,128]{2,0,1:T(8,128)S(1)} %get-tuple-element.1294), channel_id=1, source_target_pairs={{4,0},{8,4},{12,8},{16,12},{20,16},{24,20},{28,24},{5,1},{9,5},{13... | collective-permute-start | bytes 122888 | tf_op jit(solution)/shard_map/while/body/eval_jaxpr/ppermute | solution.py:31
  1098.5 931.0 %collective-permute-start.1 = (f32[5,2,128]{2,0,1:T(8,128)S(1)}, f32[5,2,128]{2,0,1:T(8,128)S(1)}, u32[]{:S(2)}, u32[]{:S(2)}) collective-permute-start(f32[5,2,128]{2,0,1:T(8,128)S(1)} %get-tuple-element.1295), channel_id=1, source_target_pairs={{1,0},{2,1},{3,2},{5,4},{6,5},{7,6},{9,8},{10,9},{11,10},{13,12},{... | collective-permute-start | bytes 15368 | tf_op jit(solution)/shard_map/while/body/eval_jaxpr/ppermute | solution.py:31
  2123.4 6.8 collective-permute-start
  2124.7 5.5 collective-permute-start.1
  (6 other events, 56.9 us)
where the time goes:
time: 2130 us
  waiting for transfers between devices  1230 us (58%)
  starting transfers between devices  707 us (33%)
  local copies, waits for them, and re-layouts  105 us (5%)
  other arithmetic  48 us (2%)
  loops' own time  22.5 us (1%)
    ppermute x44, waiting for transfers between devices, from_behind(): return lax.ppermute(block, axis, route)  1230 us
    ppermute x44, starting transfers between devices, from_behind(): return lax.ppermute(block, axis, route)  696 us
  transfers between devices with their start and end apart: 48, of which 34 were waited for; matrix products, arithmetic and copies ran while one was open for 0% of the time, Pallas kernels for 0%

commit v1 on v0

--- a/solution.py
+++ b/solution.py
@@ -1,6 +1,10 @@
+import functools
+
 import jax
 import jax.numpy as jnp
 from jax import lax
+from jax.experimental import pallas as pl
+from jax.experimental.pallas import tpu as pltpu
 from jax.sharding import PartitionSpec as P
 
 precision_high = lax.Precision.HIGHEST
@@ -243,6 +247,350 @@
     return state + flip_field(upper)
 
 
+SKEW = 2
+UNROLL = 4
+
+
+def flux_of(rho, mom, energy, direction):
+    safe = jnp.where(rho > 0.1, rho, 1.0)
+    inv_rho = 1.0 / safe
+    kinetic = mom[0] * mom[0] + mom[1] * mom[1] + mom[2] * mom[2]
+    pressure = 0.4 * (energy - 0.5 * kinetic * inv_rho)
+    velocity = mom[direction] * inv_rho
+    parts = [mom[direction]]
+    for component in range(3):
+        part = mom[component] * velocity
+        parts.append(part + pressure if component == direction else part)
+    parts.append((energy + pressure) * velocity)
+    return parts
+
+
+def spread(vector, row):
+    return jnp.broadcast_to(vector[row : row + 1, :], vector.shape)
+
+
+def step_kernel(
+    nx_dev,
+    ny_dev,
+    density,
+    momentum,
+    energy,
+    forcing,
+    coupling,
+    inverse,
+    w_ref,
+    ext,
+    flux_y,
+    pack,
+    out_a,
+    in_a,
+    grid_a,
+    grid_b,
+    out_b,
+    in_b,
+    coef,
+    halo_send,
+    halo_recv,
+    a_send,
+    a_recv,
+    b_send,
+    b_recv,
+    own_sem,
+):
+    devices = nx_dev * ny_dev
+    gx = lax.axis_index("gx")
+    gy = lax.axis_index("gy")
+    me = gy * nx_dev + gx
+    mesh_id = pl.DeviceIdType.MESH
+
+    def place(slot):
+        return (lax.rem(slot, nx_dev), lax.div(slot, nx_dev))
+
+    def other(offset):
+        return lax.rem(me + offset, devices)
+
+    barrier = pltpu.get_barrier_semaphore()
+
+    @pl.loop(1, devices)
+    def _(offset):
+        pl.semaphore_signal(barrier, inc=1, device_id=place(other(offset)), device_id_type=mesh_id)
+
+    ext[0, 2:4, 8:24, :] = density[...]
+    for component in range(3):
+        ext[1 + component, 2:4, 8:24, :] = momentum[component]
+    ext[4, 2:4, 8:24, :] = energy[...]
+
+    @pl.when(gx == 0)
+    def _():
+        ext[:, 0:2, 8:24, :] = jnp.zeros((5, 2, 16, 128), jnp.float32)
+
+    @pl.when(gx == nx_dev - 1)
+    def _():
+        ext[:, 4:6, 8:24, :] = jnp.zeros((5, 2, 16, 128), jnp.float32)
+
+    @pl.when(gy == 0)
+    def _():
+        ext[:, 2:4, 0:8, :] = jnp.zeros((5, 2, 8, 128), jnp.float32)
+
+    @pl.when(gy == ny_dev - 1)
+    def _():
+        ext[:, 2:4, 24:32, :] = jnp.zeros((5, 2, 8, 128), jnp.float32)
+
+    pl.semaphore_wait(barrier, devices - 1)
+
+    block = ext.at[:, 2:4, 8:24, :]
+    to_east = pltpu.make_async_remote_copy(
+        block, ext.at[:, 0:2, 8:24, :], halo_send.at[0], halo_recv.at[0], (gx + 1, gy), mesh_id
+    )
+    to_west = pltpu.make_async_remote_copy(
+        block, ext.at[:, 4:6, 8:24, :], halo_send.at[1], halo_recv.at[1], (gx - 1, gy), mesh_id
+    )
+    to_north = pltpu.make_async_remote_copy(
+        ext.at[:, 2:4, 16:24, :],
+        ext.at[:, 2:4, 0:8, :],
+        halo_send.at[2],
+        halo_recv.at[2],
+        (gx, gy + 1),
+        mesh_id,
+    )
+    to_south = pltpu.make_async_remote_copy(
+        ext.at[:, 2:4, 8:16, :],
+        ext.at[:, 2:4, 24:32, :],
+        halo_send.at[3],
+        halo_recv.at[3],
+        (gx, gy - 1),
+        mesh_id,
+    )
+    sides = (
+        (to_east, gx < nx_dev - 1, gx > 0),
+        (to_west, gx > 0, gx < nx_dev - 1),
+        (to_north, gy < ny_dev - 1, gy > 0),
+        (to_south, gy > 0, gy < ny_dev - 1),
+    )
+    for copy, sends, _ in sides:
+        pl.when(sends)(copy.start)
+
+    row_id = lax.broadcasted_iota(jnp.int32, (8, 128), 0)
+    inv_cols = []
+    for c in range(5):
+        column = jnp.zeros((8, 128), jnp.float32)
+        for a in range(5):
+            column = jnp.where(row_id == a, 0.25 * inverse[a, c], column)
+        inv_cols.append(column)
+        coef[4, c] = column
+    for d in range(2):
+        for b in range(5):
+            lower = inv_cols[0] * coupling[d, 0, b]
+            upper = inv_cols[0] * coupling[d, b, 0]
+            for c in range(1, 5):
+                lower = lower + inv_cols[c] * coupling[d, c, b]
+                upper = upper + inv_cols[c] * coupling[d, b, c]
+            coef[d, b] = lower
+            coef[2 + d, b] = upper
+    grid_a[...] = jnp.zeros(grid_a.shape, jnp.float32)
+    grid_b[...] = jnp.zeros(grid_b.shape, jnp.float32)
+
+    rho = density[...]
+    mom = [momentum[c] for c in range(3)]
+    en = energy[...]
+    inv_rho = 1.0 / rho
+    vel = [m * inv_rho for m in mom]
+    inv_scale = 1.0 / (1.0 + vel[0] * vel[0] + vel[1] * vel[1] + vel[2] * vel[2])
+    own = [rho] + mom + [en]
+    flux_z = flux_of(rho, mom, en, 2)
+    lane3 = lax.broadcasted_iota(jnp.int32, (2, 16, 128), 2)
+
+    def from_z(field, offset):
+        moved = pltpu.roll(field.reshape(32, 128), (-offset) % 128, 1).reshape(2, 16, 128)
+        inside = (lane3 < 128 - offset) if offset > 0 else (lane3 >= -offset)
+        return jnp.where(inside, moved, 0.0)
+
+    rsd = []
+    for f in range(5):
+        total = forcing[f] - (18.0 * dissipation) * own[f]
+        total = total + from_z(4.0 * dissipation * own[f] - 0.5 * flux_z[f], 1)
+        total = total + from_z(4.0 * dissipation * own[f] + 0.5 * flux_z[f], -1)
+        total = total - dissipation * (from_z(own[f], 2) + from_z(own[f], -2))
+        rsd.append(total)
+
+    for copy, _, receives in sides:
+        pl.when(receives)(copy.wait_recv)
+
+    wide = [ext[f, 1:5, 8:24, :] for f in range(5)]
+    flux_x = flux_of(wide[0], wide[1:4], wide[4], 0)
+    tall = [ext[f, 2:4, :, :] for f in range(5)]
+    for f, part in enumerate(flux_of(tall[0], tall[1:4], tall[4], 1)):
+        flux_y[f] = part
+    for f in range(5):
+        total = rsd[f] - 0.5 * (flux_x[f][2:4] - flux_x[f][0:2])
+        total = total - 0.5 * (flux_y[f, :, 9:25, :] - flux_y[f, :, 7:23, :])
+        near = (wide[f][0:2] + wide[f][2:4]) + (ext[f, 2:4, 7:23, :] + ext[f, 2:4, 9:25, :])
+        far = (ext[f, 0:2, 8:24, :] + ext[f, 4:6, 8:24, :]) + (
+            ext[f, 2:4, 6:22, :] + ext[f, 2:4, 10:26, :]
+        )
+        rsd[f] = total + dissipation * (4.0 * near - far)
+
+    fields = []
+    for a in range(5):
+        total = inverse[a, 0] * rsd[0]
+        for b in range(1, 5):
+            total = total + inverse[a, b] * rsd[b]
+        fields.append(total * inv_scale)
+    fields += [vel[0], vel[1], inv_scale]
+
+    for xl in range(2):
+        for f in range(8):
+            pack[pl.ds(xl * 128 + f, 16, stride=8), :] = fields[f][xl]
+        turned = pack[xl * 128 : (xl + 1) * 128, :].T
+        for part in range(4):
+            out_a[pl.ds(xl * 4 + part, 32, stride=8), :] = turned[part * 32 : (part + 1) * 32]
+
+    def tile(ref, slot):
+        return ref.at[pl.ds(pl.multiple_of(slot * 8, 8), 8), :]
+
+    def exchange(source, target, send, recv):
+        def to_slot(offset):
+            slot = other(offset)
+            return pltpu.make_async_remote_copy(
+                tile(source, slot), tile(target, me), send.at[slot], recv.at[me], place(slot), mesh_id
+            )
+
+        def from_slot(offset):
+            slot = other(offset)
+            return pltpu.make_async_remote_copy(
+                tile(source, slot), tile(target, slot), send.at[slot], recv.at[slot], place(slot), mesh_id
+            )
+
+        pl.loop(1, devices)(lambda offset: to_slot(offset).start())
+        mine = pltpu.make_async_copy(tile(source, me), tile(target, me), own_sem)
+        mine.start()
+        mine.wait()
+        pl.loop(1, devices)(lambda offset: from_slot(offset).wait_recv())
+
+        return lambda: pl.loop(1, devices)(lambda offset: to_slot(offset).wait_send())
+
+    finish_a = exchange(out_a, in_a, a_send, a_recv)
+
+    lane = lax.broadcasted_iota(jnp.int32, (128, 128), 1)
+    low = lane < 64
+    front = 8 * SKEW
+    for pair in range(ny_dev // 2):
+        turned = in_a[pair * 128 : (pair + 1) * 128, :].T
+        first = front + pair * 32
+        grid_a[first : first + 16] = jnp.where(low, turned, 0.0).reshape(16, 8, 128)
+        turned = pltpu.roll(turned, 64, 1)
+        grid_a[first + 16 : first + 32] = jnp.where(low, turned, 0.0).reshape(16, 8, 128)
+
+    extent_y = 16 * ny_dev
+    lane_x = lax.broadcasted_iota(jnp.int32, (1, 8, 128), 2) // 4
+    buffers = (grid_a, grid_b)
+    for bit in range(4):
+        source, target = buffers[bit % 2], buffers[1 - bit % 2]
+        shift = SKEW << bit
+        rows = extent_y + SKEW * ((2 << bit) - 1)
+        odd = (lane_x // (1 << bit)) % 2 == 1
+        target[front : front + rows] = jnp.where(
+            odd, source[front - shift : front - shift + rows], source[front : front + rows]
+        )
+
+    steps = extent_y + 15 * SKEW
+    steps = -(-steps // UNROLL) * UNROLL
+    zero = jnp.zeros((8, 128), jnp.float32)
+
+    def run_sweep(first_coef, sign, roll_by, row_of):
+        mat_x = [coef[first_coef, b] for b in range(5)]
+        mat_y = [coef[first_coef + 1, b] for b in range(5)]
+        mat_i = [coef[4, b] for b in range(5)]
+
+        def advance(index, carry):
+            south, queue = carry[0], list(carry[1:])
+            for inner in range(UNROLL):
+                row = row_of(index * UNROLL + inner)
+                cells = grid_a[row]
+                cells = cells - spread(cells, 7) * (south + queue.pop(0))
+                grid_a[row] = cells
+                speed_x = sign * spread(cells, 5)
+                speed_y = sign * spread(cells, 6)
+                values = [spread(cells, b) for b in range(5)]
+                terms = [(mat_y[b] + speed_y * mat_i[b]) * values[b] for b in range(5)]
+                south = ((terms[0] + terms[1]) + (terms[2] + terms[3])) + terms[4]
+                terms = [(mat_x[b] + speed_x * mat_i[b]) * values[b] for b in range(5)]
+                west = ((terms[0] + terms[1]) + (terms[2] + terms[3])) + terms[4]
+                queue.append(pltpu.roll(west, roll_by, 1))
+            return (south, *queue)
+
+        lax.fori_loop(0, steps // UNROLL, advance, (zero,) * (1 + SKEW))
+
+    run_sweep(0, 1.0, 4, lambda step: front + step)
+    run_sweep(2, -1.0, 124, lambda step: front + steps - 1 - step)
+
+    for turn, bit in enumerate((3, 2, 1, 0)):
+        source, target = buffers[turn % 2], buffers[1 - turn % 2]
+        shift = SKEW << bit
+        rows = extent_y + SKEW * ((1 << bit) - 1)
+        odd = (lane_x // (1 << bit)) % 2 == 1
+        target[front : front + rows] = jnp.where(
+            odd, source[front + shift : front + shift + rows], source[front : front + rows]
+        )
+
+    for pair in range(ny_dev // 2):
+        first = front + pair * 32
+        left = grid_a[first : first + 16].reshape(128, 128)
+        right = pltpu.roll(grid_a[first + 16 : first + 32].reshape(128, 128), 64, 1)
+        out_b[pair * 128 : (pair + 1) * 128, :] = jnp.where(low, left, right).T
+
+    finish_b = exchange(out_b, in_b, b_send, b_recv)
+
+    for xl in range(2):
+        planes = [in_b[pl.ds(xl * 4 + part, 32, stride=8), :] for part in range(4)]
+        pack[xl * 128 : (xl + 1) * 128, :] = jnp.concatenate(planes, axis=0).T
+        for f in range(5):
+            w_ref[f, xl] = pack[pl.ds(xl * 128 + f, 16, stride=8), :]
+
+    for copy, sends, _ in sides:
+        pl.when(sends)(copy.wait_send)
+    finish_a()
+    finish_b()
+
+
+def kernel_shards(nx_dev, ny_dev, density, momentum, energy, forcing, coupling, inverse):
+    devices = nx_dev * ny_dev
+    grid_rows = 8 * SKEW + 16 * ny_dev + 15 * SKEW + UNROLL
+    vmem = pl.BlockSpec(memory_space=pltpu.VMEM)
+    smem = pl.BlockSpec(memory_space=pltpu.SMEM)
+    change = pl.pallas_call(
+        functools.partial(step_kernel, nx_dev, ny_dev),
+        out_shape=jax.ShapeDtypeStruct((5, 2, 16, 128), jnp.float32),
+        in_specs=[vmem] * 4 + [smem] * 2,
+        out_specs=vmem,
+        scratch_shapes=[
+            pltpu.VMEM((5, 6, 32, 128), jnp.float32),
+            pltpu.VMEM((5, 2, 32, 128), jnp.float32),
+            pltpu.VMEM((256, 128), jnp.float32),
+            pltpu.VMEM((8 * devices, 128), jnp.float32),
+            pltpu.VMEM((8 * devices, 128), jnp.float32),
+            pltpu.VMEM((grid_rows, 8, 128), jnp.float32),
+            pltpu.VMEM((grid_rows, 8, 128), jnp.float32),
+            pltpu.VMEM((8 * devices, 128), jnp.float32),
+            pltpu.VMEM((8 * devices, 128), jnp.float32),
+            pltpu.VMEM((5, 5, 8, 128), jnp.float32),
+            pltpu.SemaphoreType.DMA((4,)),
+            pltpu.SemaphoreType.DMA((4,)),
+            pltpu.SemaphoreType.DMA((devices,)),
+            pltpu.SemaphoreType.DMA((devices,)),
+            pltpu.SemaphoreType.DMA((devices,)),
+            pltpu.SemaphoreType.DMA((devices,)),
+            pltpu.SemaphoreType.DMA,
+        ],
+        compiler_params=pltpu.CompilerParams(
+            collective_id=0, has_side_effects=True, vmem_limit_bytes=32 * 1024 * 1024
+        ),
+        name="lu_step",
+    )(density, momentum, energy, forcing, coupling, inverse)
+    state = jnp.concatenate([density[None], momentum, energy[None]], axis=0)
+    return state + change
+
+
 def solution(mesh):
     placed = (
         P("gx", "gy", None),
@@ -252,6 +600,13 @@
         P(),
         P(),
     )
+    nx_dev, ny_dev = mesh.shape["gx"], mesh.shape["gy"]
+
+    def local(*args):
+        if args[0].shape == (2, 16, 128) and (nx_dev, ny_dev) == (8, 4):
+            return kernel_shards(nx_dev, ny_dev, *args)
+        return shards(*args)
+
     return jax.shard_map(
-        shards, mesh=mesh, in_specs=placed, out_specs=P(None, "gx", "gy", None), check_vma=False
-    )
+        local, mesh=mesh, in_specs=placed, out_specs=P(None, "gx", "gy", None), check_vma=False
+    )

time: 2130 us -> 37.3 us (0.02)
  waiting for transfers between devices: 1230 us -> 0 us
  starting transfers between devices: 707 us -> 0 us
  local copies, waits for them, and re-layouts: 105 us -> 3.8 us
  other arithmetic: 48 us -> 0.65 us
  Pallas kernels: 0 us -> 32.4 us
  loops' own time: 22.5 us -> 0 us
    ppermute x48 -> x0, waiting for transfers between devices: 1230 us -> none  [the longest x44 1230 us: from_behind(): return lax.ppermute(block, axis, route)]
    ppermute x48 -> x0, starting transfers between devices: 707 us -> none  [the longest x44 696 us: from_behind(): return lax.ppermute(block, axis, route)]
    gather x138 -> x0, local copies, waits for them, and re-layouts: 80.2 us -> none  [the longest x34 19.8 us: step(): vel_x[row_ids, col_clip]]
    pallas_call x0 -> x1, Pallas kernels: none -> 32.4 us  [kernel_shards(): pl.pallas_call(functools.partial(step_kernel, nx_dev, ny_dev), out_shape=...]
    another operation x26 -> x0, loops' own time: 22.5 us -> none  [the longest x2 21.5 us: sweep(): _, diagonals = lax.scan(step, (initial, initial), diag_ids)]
    concatenate x39 -> x0, other arithmetic: 21.4 us -> none  [the longest x34 20.2 us: step(): cell_lead = lead_term[:, row_ids, col_clip]]
  transfers between devices with their start and end apart: 48 -> 0, of which waited for: 34 -> 0; matrix products, arithmetic and copies ran while one was open for 0% -> 0% of each run, Pallas kernels for 0% -> 0%
where the time goes in v1:
time: 37.3 us; the launch traced here: 36.9 us
  Pallas kernels  32.4 us (87%)
  local copies, waits for them, and re-layouts  3.8 us (10%)
  other arithmetic  0.65 us (2%)
    pallas_call x1, Pallas kernels, kernel_shards(): pl.pallas_call(functools.partial(step_kernel, nx_dev, ny_dev), out_shape=...  32.4 us
    unnamed x11, local copies, waits for them, and re-layouts  3.8 us

profile of v1, /device:TPU:0, one launch (start us, length us, event | category | flops | bytes accessed | tf_op | source)
XLA Modules:
  0.0 36.9 jit_solution(5766155147786145790)
XLA Ops:
  0.0 0.0 copy-start.2
  0.0 0.7 %copy.7.coupling = f32[2,5,5]{2,1,0:T(8,128)S(1)} copy(f32[2,5,5]{2,0,1:T(2,128)} %param.10) | data formatting | bytes 400 | tf_op args[4]
  0.7 0.0 copy-done.2
  0.7 0.0 copy-start
  0.7 0.8 %copy-done = f32[3,2,16,128]{3,2,1,0:T(8,128)S(1)} copy-done((f32[3,2,16,128]{3,2,1,0:T(8,128)S(1)}, f32[3,2,16,128]{3,2,1,0:T(8,128)}, u32[]{:S(2)}) %copy-start) | copy-done | bytes 49176
  1.5 0.0 copy-start.1
  1.5 0.9 %copy-done.1 = f32[5,2,16,128]{3,2,1,0:T(8,128)S(1)} copy-done((f32[5,2,16,128]{3,2,1,0:T(8,128)S(1)}, f32[5,2,16,128]{3,2,1,0:T(8,128)}, u32[]{:S(2)}) %copy-start.1) | copy-done | bytes 81944
  2.4 0.0 copy-start.3
  2.4 0.7 %copy-done.3 = f32[2,16,128]{2,1,0:T(8,128)S(1)} copy-done((f32[2,16,128]{2,1,0:T(8,128)S(1)}, f32[2,16,128]{2,1,0:T(8,128)}, u32[]{:S(2)}) %copy-start.3) | copy-done | bytes 16408
  3.1 0.0 copy-start.4
  3.1 0.7 %copy-done.4 = f32[5,5]{1,0:T(8,128)S(1)} copy-done((f32[5,5]{1,0:T(8,128)S(1)}, f32[5,5]{1,0:T(8,128)}, u32[]{:S(2)}) %copy-start.4) | copy-done | bytes 124
  3.8 32.4 %lu_step.1 = f32[5,2,16,128]{3,2,1,0:T(8,128)S(1)} custom-call(f32[2,16,128]{2,1,0:T(8,128)S(1)} %copy-done.2, f32[3,2,16,128]{3,2,1,0:T(8,128)S(1)} %copy-done, f32[2,16,128]{2,1,0:T(8,128)S(1)} %copy-done.3, f32[5,2,16,128]{3,2,1,0:T(8,128)S(1)} %copy-done.1, f32[2,5,5]{2,1,0:T(8,128)S(1)} %copy.7.coupling, f32[5,5]{1,0:T(8,128)S(1)} %copy-done.4), custom_call_target="tpu_custom_call" | custom-call | tf_op jit(solution)/shard_map/lu_step/pallas_call | solution.py:561
  36.2 0.6 %maximum_add_fusion = f32[5,2,16,128]{3,2,1,0:T(8,128)} fusion(f32[5,2,16,128]{3,2,1,0:T(8,128)S(1)} %lu_step.1, f32[1,2,16,128]{3,2,1,0:T(8,128)S(1)} %bitcast.3, f32[3,2,16,128]{3,2,1,0:T(8,128)S(1)} %copy-done, f32[1,2,16,128]{3,2,1,0:T(8,128)S(1)} %bitcast.2), kind=kLoop, calls=%fused_computation | loop fusion | flops 61440 | bytes 245760 | tf_op jit(solution)/shard_map/add | solution.py:591
Async XLA Ops:
  0.0 0.7 %copy-start.2 = (f32[2,16,128]{2,1,0:T(8,128)S(1)}, f32[2,16,128]{2,1,0:T(8,128)}, u32[]{:S(2)}) copy-start(f32[2,16,128]{2,1,0:T(8,128)} %density.1) | copy-start | bytes 49156
  0.7 0.8 %copy-start = (f32[3,2,16,128]{3,2,1,0:T(8,128)S(1)}, f32[3,2,16,128]{3,2,1,0:T(8,128)}, u32[]{:S(2)}) copy-start(f32[3,2,16,128]{3,2,1,0:T(8,128)} %momentum.1) | copy-start | bytes 147460
  1.5 0.9 %copy-start.1 = (f32[5,2,16,128]{3,2,1,0:T(8,128)S(1)}, f32[5,2,16,128]{3,2,1,0:T(8,128)}, u32[]{:S(2)}) copy-start(f32[5,2,16,128]{3,2,1,0:T(8,128)} %forcing.1) | copy-start | bytes 245764
  2.4 0.7 %copy-start.3 = (f32[2,16,128]{2,1,0:T(8,128)S(1)}, f32[2,16,128]{2,1,0:T(8,128)}, u32[]{:S(2)}) copy-start(f32[2,16,128]{2,1,0:T(8,128)} %energy.1) | copy-start | bytes 49156
  3.1 0.7 %copy-start.4 = (f32[5,5]{1,0:T(8,128)S(1)}, f32[5,5]{1,0:T(8,128)}, u32[]{:S(2)}) copy-start(f32[5,5]{1,0:T(8,128)} %inverse.1) | copy-start | bytes 304

commit v2 on v1

--- a/solution.py
+++ b/solution.py
@@ -247,8 +247,8 @@
     return state + flip_field(upper)
 
 
-SKEW = 2
-UNROLL = 4
+SKEW = 4
+UNROLL = 8
 
 
 def flux_of(rho, mom, energy, direction):
@@ -272,14 +272,17 @@
 def step_kernel(
     nx_dev,
     ny_dev,
-    density,
-    momentum,
-    energy,
+    density_hbm,
+    momentum_hbm,
+    energy_hbm,
+    forcing_hbm,
+    coupling_hbm,
+    inverse_hbm,
+    w_ref,
+    ext,
     forcing,
     coupling,
     inverse,
-    w_ref,
-    ext,
     flux_y,
     pack,
     out_a,
@@ -296,6 +299,7 @@
     b_send,
     b_recv,
     own_sem,
+    load_sem,
 ):
     devices = nx_dev * ny_dev
     gx = lax.axis_index("gx")
@@ -309,17 +313,29 @@
     def other(offset):
         return lax.rem(me + offset, devices)
 
+    middle = (slice(2, 4), slice(8, 24), slice(None))
+    loads = [
+        pltpu.make_async_copy(source, target, load_sem.at[number])
+        for number, (source, target) in enumerate(
+            (
+                (density_hbm, ext.at[(0,) + middle]),
+                (momentum_hbm, ext.at[(slice(1, 4),) + middle]),
+                (energy_hbm, ext.at[(4,) + middle]),
+                (forcing_hbm, forcing),
+                (coupling_hbm, coupling),
+                (inverse_hbm, inverse),
+            )
+        )
+    ]
+    for load in loads:
+        load.start()
+
     barrier = pltpu.get_barrier_semaphore()
 
     @pl.loop(1, devices)
     def _(offset):
         pl.semaphore_signal(barrier, inc=1, device_id=place(other(offset)), device_id_type=mesh_id)
 
-    ext[0, 2:4, 8:24, :] = density[...]
-    for component in range(3):
-        ext[1 + component, 2:4, 8:24, :] = momentum[component]
-    ext[4, 2:4, 8:24, :] = energy[...]
-
     @pl.when(gx == 0)
     def _():
         ext[:, 0:2, 8:24, :] = jnp.zeros((5, 2, 16, 128), jnp.float32)
@@ -336,40 +352,8 @@
     def _():
         ext[:, 2:4, 24:32, :] = jnp.zeros((5, 2, 8, 128), jnp.float32)
 
-    pl.semaphore_wait(barrier, devices - 1)
-
-    block = ext.at[:, 2:4, 8:24, :]
-    to_east = pltpu.make_async_remote_copy(
-        block, ext.at[:, 0:2, 8:24, :], halo_send.at[0], halo_recv.at[0], (gx + 1, gy), mesh_id
-    )
-    to_west = pltpu.make_async_remote_copy(
-        block, ext.at[:, 4:6, 8:24, :], halo_send.at[1], halo_recv.at[1], (gx - 1, gy), mesh_id
-    )
-    to_north = pltpu.make_async_remote_copy(
-        ext.at[:, 2:4, 16:24, :],
-        ext.at[:, 2:4, 0:8, :],
-        halo_send.at[2],
-        halo_recv.at[2],
-        (gx, gy + 1),
-        mesh_id,
-    )
-    to_south = pltpu.make_async_remote_copy(
-        ext.at[:, 2:4, 8:16, :],
-        ext.at[:, 2:4, 24:32, :],
-        halo_send.at[3],
-        halo_recv.at[3],
-        (gx, gy - 1),
-        mesh_id,
-    )
-    sides = (
-        (to_east, gx < nx_dev - 1, gx > 0),
-        (to_west, gx > 0, gx < nx_dev - 1),
-        (to_north, gy < ny_dev - 1, gy > 0),
-        (to_south, gy > 0, gy < ny_dev - 1),
-    )
-    for copy, sends, _ in sides:
-        pl.when(sends)(copy.start)
-
+    loads[4].wait()
+    loads[5].wait()
     row_id = lax.broadcasted_iota(jnp.int32, (8, 128), 0)
     inv_cols = []
     for c in range(5):
@@ -380,19 +364,54 @@
         coef[4, c] = column
     for d in range(2):
         for b in range(5):
-            lower = inv_cols[0] * coupling[d, 0, b]
-            upper = inv_cols[0] * coupling[d, b, 0]
+            lower = inv_cols[0] * coupling[0, d, b]
+            upper = inv_cols[0] * coupling[b, d, 0]
             for c in range(1, 5):
-                lower = lower + inv_cols[c] * coupling[d, c, b]
-                upper = upper + inv_cols[c] * coupling[d, b, c]
+                lower = lower + inv_cols[c] * coupling[c, d, b]
+                upper = upper + inv_cols[c] * coupling[b, d, c]
             coef[d, b] = lower
             coef[2 + d, b] = upper
     grid_a[...] = jnp.zeros(grid_a.shape, jnp.float32)
     grid_b[...] = jnp.zeros(grid_b.shape, jnp.float32)
 
-    rho = density[...]
-    mom = [momentum[c] for c in range(3)]
-    en = energy[...]
+    for load in loads[:3]:
+        load.wait()
+    pl.semaphore_wait(barrier, devices - 1)
+
+    block = ext.at[:, 2:4, 8:24, :]
+    to_east = pltpu.make_async_remote_copy(
+        block, ext.at[:, 0:2, 8:24, :], halo_send.at[0], halo_recv.at[0], (gx + 1, gy), mesh_id
+    )
+    to_west = pltpu.make_async_remote_copy(
+        block, ext.at[:, 4:6, 8:24, :], halo_send.at[1], halo_recv.at[1], (gx - 1, gy), mesh_id
+    )
+    to_north = pltpu.make_async_remote_copy(
+        ext.at[:, 2:4, 16:24, :],
+        ext.at[:, 2:4, 0:8, :],
+        halo_send.at[2],
+        halo_recv.at[2],
+        (gx, gy + 1),
+        mesh_id,
+    )
+    to_south = pltpu.make_async_remote_copy(
+        ext.at[:, 2:4, 8:16, :],
+        ext.at[:, 2:4, 24:32, :],
+        halo_send.at[3],
+        halo_recv.at[3],
+        (gx, gy - 1),
+        mesh_id,
+    )
+    sides = (
+        (to_east, gx < nx_dev - 1, gx > 0),
+        (to_west, gx > 0, gx < nx_dev - 1),
+        (to_north, gy < ny_dev - 1, gy > 0),
+        (to_south, gy > 0, gy < ny_dev - 1),
+    )
+    for copy, sends, _ in sides:
+        pl.when(sends)(copy.start)
+
+    loads[3].wait()
+    rho, *mom, en = [ext[f, 2:4, 8:24, :] for f in range(5)]
     inv_rho = 1.0 / rho
     vel = [m * inv_rho for m in mom]
     inv_scale = 1.0 / (1.0 + vel[0] * vel[0] + vel[1] * vel[1] + vel[2] * vel[2])
@@ -449,25 +468,22 @@
         return ref.at[pl.ds(pl.multiple_of(slot * 8, 8), 8), :]
 
     def exchange(source, target, send, recv):
-        def to_slot(offset):
+        @pl.loop(1, devices)
+        def _(offset):
             slot = other(offset)
-            return pltpu.make_async_remote_copy(
-                tile(source, slot), tile(target, me), send.at[slot], recv.at[me], place(slot), mesh_id
-            )
-
-        def from_slot(offset):
-            slot = other(offset)
-            return pltpu.make_async_remote_copy(
-                tile(source, slot), tile(target, slot), send.at[slot], recv.at[slot], place(slot), mesh_id
-            )
-
-        pl.loop(1, devices)(lambda offset: to_slot(offset).start())
+            pltpu.make_async_remote_copy(
+                tile(source, slot), tile(target, me), send, recv, place(slot), mesh_id
+            ).start()
+
         mine = pltpu.make_async_copy(tile(source, me), tile(target, me), own_sem)
         mine.start()
         mine.wait()
-        pl.loop(1, devices)(lambda offset: from_slot(offset).wait_recv())
-
-        return lambda: pl.loop(1, devices)(lambda offset: to_slot(offset).wait_send())
+        rows = pl.ds(0, 8 * (devices - 1))
+        whole = pltpu.make_async_remote_copy(
+            source.at[rows, :], target.at[rows, :], send, recv, place(other(1)), mesh_id
+        )
+        whole.wait_recv()
+        return whole.wait_send
 
     finish_a = exchange(out_a, in_a, a_send, a_recv)
 
@@ -503,23 +519,24 @@
         mat_i = [coef[4, b] for b in range(5)]
 
         def advance(index, carry):
-            south, queue = carry[0], list(carry[1:])
+            first, second, third, *queue = carry
             for inner in range(UNROLL):
                 row = row_of(index * UNROLL + inner)
+                after = spread(grid_a[row_of(index * UNROLL + inner + 1)], 7)
                 cells = grid_a[row]
-                cells = cells - spread(cells, 7) * (south + queue.pop(0))
-                grid_a[row] = cells
                 speed_x = sign * spread(cells, 5)
                 speed_y = sign * spread(cells, 6)
+                cells = cells - spread(cells, 7) * pltpu.roll(queue.pop(0), roll_by, 1)
+                cells = ((cells - first) - second) - third
+                grid_a[row] = cells
                 values = [spread(cells, b) for b in range(5)]
-                terms = [(mat_y[b] + speed_y * mat_i[b]) * values[b] for b in range(5)]
-                south = ((terms[0] + terms[1]) + (terms[2] + terms[3])) + terms[4]
+                terms = [((mat_y[b] + speed_y * mat_i[b]) * after) * values[b] for b in range(5)]
+                first, second, third = terms[0], terms[1] + terms[2], terms[3] + terms[4]
                 terms = [(mat_x[b] + speed_x * mat_i[b]) * values[b] for b in range(5)]
-                west = ((terms[0] + terms[1]) + (terms[2] + terms[3])) + terms[4]
-                queue.append(pltpu.roll(west, roll_by, 1))
-            return (south, *queue)
-
-        lax.fori_loop(0, steps // UNROLL, advance, (zero,) * (1 + SKEW))
+                queue.append(((terms[0] + terms[1]) + (terms[2] + terms[3])) + terms[4])
+            return (first, second, third, *queue)
+
+        lax.fori_loop(0, steps // UNROLL, advance, (zero,) * (3 + SKEW))
 
     run_sweep(0, 1.0, 4, lambda step: front + step)
     run_sweep(2, -1.0, 124, lambda step: front + steps - 1 - step)
@@ -557,14 +574,16 @@
     devices = nx_dev * ny_dev
     grid_rows = 8 * SKEW + 16 * ny_dev + 15 * SKEW + UNROLL
     vmem = pl.BlockSpec(memory_space=pltpu.VMEM)
-    smem = pl.BlockSpec(memory_space=pltpu.SMEM)
     change = pl.pallas_call(
         functools.partial(step_kernel, nx_dev, ny_dev),
         out_shape=jax.ShapeDtypeStruct((5, 2, 16, 128), jnp.float32),
-        in_specs=[vmem] * 4 + [smem] * 2,
+        in_specs=[pl.BlockSpec(memory_space=pltpu.HBM)] * 6,
         out_specs=vmem,
         scratch_shapes=[
             pltpu.VMEM((5, 6, 32, 128), jnp.float32),
+            pltpu.VMEM((5, 2, 16, 128), jnp.float32),
+            pltpu.SMEM((5, 2, 5), jnp.float32),
+            pltpu.SMEM((5, 5), jnp.float32),
             pltpu.VMEM((5, 2, 32, 128), jnp.float32),
             pltpu.VMEM((256, 128), jnp.float32),
             pltpu.VMEM((8 * devices, 128), jnp.float32),
@@ -576,17 +595,18 @@
             pltpu.VMEM((5, 5, 8, 128), jnp.float32),
             pltpu.SemaphoreType.DMA((4,)),
             pltpu.SemaphoreType.DMA((4,)),
-            pltpu.SemaphoreType.DMA((devices,)),
-            pltpu.SemaphoreType.DMA((devices,)),
-            pltpu.SemaphoreType.DMA((devices,)),
-            pltpu.SemaphoreType.DMA((devices,)),
             pltpu.SemaphoreType.DMA,
+            pltpu.SemaphoreType.DMA,
+            pltpu.SemaphoreType.DMA,
+            pltpu.SemaphoreType.DMA,
+            pltpu.SemaphoreType.DMA,
+            pltpu.SemaphoreType.DMA((6,)),
         ],
         compiler_params=pltpu.CompilerParams(
-            collective_id=0, has_side_effects=True, vmem_limit_bytes=32 * 1024 * 1024
+            collective_id=0, has_side_effects=True, vmem_limit_bytes=60 * 1024 * 1024
         ),
         name="lu_step",
-    )(density, momentum, energy, forcing, coupling, inverse)
+    )(density, momentum, energy, forcing, jnp.swapaxes(coupling, 0, 1), inverse)
     state = jnp.concatenate([density[None], momentum, energy[None]], axis=0)
     return state + change
 

time: 37.3 us -> 29.8 us (0.80)
  Pallas kernels: 32.4 us -> 28 us
  local copies, waits for them, and re-layouts: 3.8 us -> 0.01 us
  other arithmetic: 0.65 us -> 1.54 us
    pallas_call x1, Pallas kernels: 32.4 us -> 28 us  [kernel_shards(): pl.pallas_call(functools.partial(step_kernel, nx_dev, ny_dev), out_shape=...]
    unnamed x11 -> x6, local copies, waits for them, and re-layouts: 3.8 us -> 0.01 us
    add x1, other arithmetic: 0.65 us -> 1.54 us  [kernel_shards(): return state + change]
where the time goes in v2:
time: 29.8 us; the launch traced here: 29.6 us
  Pallas kernels  28 us (94%)
  other arithmetic  1.54 us (5%)
    pallas_call x1, Pallas kernels, kernel_shards(): pl.pallas_call(functools.partial(step_kernel, nx_dev, ny_dev), out_shape=...  28 us
    add x1, other arithmetic, kernel_shards(): return state + change  1.54 us

profile of v2, /device:TPU:0, one launch (start us, length us, event | category | flops | bytes accessed | tf_op | source)
XLA Modules:
  0.0 29.6 jit_solution(3431241040077771849)
XLA Ops:
  0.0 0.0 copy-start
  0.0 0.0 copy-start.1
  0.0 0.0 copy-start.2
  0.0 28.0 %lu_step.1 = f32[5,2,16,128]{3,2,1,0:T(8,128)} custom-call(f32[2,16,128]{2,1,0:T(8,128)} %density_hbm.1, f32[3,2,16,128]{3,2,1,0:T(8,128)} %momentum_hbm.1, f32[2,16,128]{2,1,0:T(8,128)} %energy_hbm.1, f32[5,2,16,128]{3,2,1,0:T(8,128)} %forcing_hbm.1, f32[5,2,5]{2,1,0:T(2,128)} %bitcast.5, f32[5,5]{1,0:T(8,128)} %inverse_hbm.1), custom_call_target="tpu_custom_call" | custom-call | tf_op jit(solution)/shard_map/lu_step/pallas_call | solution.py:577
  28.0 0.0 copy-done
  28.0 0.0 copy-done.1
  28.0 0.0 copy-done.2
  28.0 1.5 %maximum_add_fusion = f32[5,2,16,128]{3,2,1,0:T(8,128)} fusion(f32[5,2,16,128]{3,2,1,0:T(8,128)} %lu_step.1, f32[1,2,16,128]{3,2,1,0:T(8,128)S(1)} %bitcast.4, f32[3,2,16,128]{3,2,1,0:T(8,128)S(1)} %copy-done, f32[1,2,16,128]{3,2,1,0:T(8,128)S(1)} %bitcast.3), kind=kLoop, calls=%fused_computation | loop fusion | flops 61440 | bytes 245760 | tf_op jit(solution)/shard_map/add | solution.py:611
Async XLA Ops:
  0.0 28.0 %copy-start = (f32[3,2,16,128]{3,2,1,0:T(8,128)S(1)}, f32[3,2,16,128]{3,2,1,0:T(8,128)}, u32[]{:S(2)}) copy-start(f32[3,2,16,128]{3,2,1,0:T(8,128)} %momentum_hbm.1) | copy-start | bytes 147460
  0.0 28.0 %copy-start.1 = (f32[2,16,128]{2,1,0:T(8,128)S(1)}, f32[2,16,128]{2,1,0:T(8,128)}, u32[]{:S(2)}) copy-start(f32[2,16,128]{2,1,0:T(8,128)} %density_hbm.1) | copy-start | bytes 49156
  0.0 28.0 %copy-start.2 = (f32[2,16,128]{2,1,0:T(8,128)S(1)}, f32[2,16,128]{2,1,0:T(8,128)}, u32[]{:S(2)}) copy-start(f32[2,16,128]{2,1,0:T(8,128)} %energy_hbm.1) | copy-start | bytes 49156

commit v3 on v2

--- a/solution.py
+++ b/solution.py
@@ -248,7 +248,7 @@
 
 
 SKEW = 4
-UNROLL = 8
+UNROLL = 16
 
 
 def flux_of(rho, mom, energy, direction):

time: 29.8 us -> 29.4 us (0.987)
  Pallas kernels: 28 us -> 27.6 us
    pallas_call x1, Pallas kernels: 28 us -> 27.6 us  [kernel_shards(): pl.pallas_call(functools.partial(step_kernel, nx_dev, ny_dev), out_shape=...]
where the time goes in v3:
time: 29.4 us; the launch traced here: 29.2 us
  Pallas kernels  27.6 us (94%)
  other arithmetic  1.54 us (5%)
    pallas_call x1, Pallas kernels, kernel_shards(): pl.pallas_call(functools.partial(step_kernel, nx_dev, ny_dev), out_shape=...  27.6 us
    add x1, other arithmetic, kernel_shards(): return state + change  1.54 us

profile of v3, /device:TPU:0, one launch (start us, length us, event | category | flops | bytes accessed | tf_op | source)
XLA Modules:
  0.0 29.2 jit_solution(4982044822646044091)
XLA Ops:
  0.0 0.0 copy-start
  0.0 0.0 copy-start.1
  0.0 0.0 copy-start.2
  0.0 27.6 %lu_step.1 = f32[5,2,16,128]{3,2,1,0:T(8,128)} custom-call(f32[2,16,128]{2,1,0:T(8,128)} %density_hbm.1, f32[3,2,16,128]{3,2,1,0:T(8,128)} %momentum_hbm.1, f32[2,16,128]{2,1,0:T(8,128)} %energy_hbm.1, f32[5,2,16,128]{3,2,1,0:T(8,128)} %forcing_hbm.1, f32[5,2,5]{2,1,0:T(2,128)} %bitcast.5, f32[5,5]{1,0:T(8,128)} %inverse_hbm.1), custom_call_target="tpu_custom_call" | custom-call | tf_op jit(solution)/shard_map/lu_step/pallas_call | solution.py:577
  27.6 0.0 copy-done
  27.6 0.0 copy-done.1
  27.7 0.0 copy-done.2
  27.7 1.5 %maximum_add_fusion = f32[5,2,16,128]{3,2,1,0:T(8,128)} fusion(f32[5,2,16,128]{3,2,1,0:T(8,128)} %lu_step.1, f32[1,2,16,128]{3,2,1,0:T(8,128)S(1)} %bitcast.4, f32[3,2,16,128]{3,2,1,0:T(8,128)S(1)} %copy-done, f32[1,2,16,128]{3,2,1,0:T(8,128)S(1)} %bitcast.3), kind=kLoop, calls=%fused_computation | loop fusion | flops 61440 | bytes 245760 | tf_op jit(solution)/shard_map/add | solution.py:611
Async XLA Ops:
  0.0 27.6 %copy-start = (f32[3,2,16,128]{3,2,1,0:T(8,128)S(1)}, f32[3,2,16,128]{3,2,1,0:T(8,128)}, u32[]{:S(2)}) copy-start(f32[3,2,16,128]{3,2,1,0:T(8,128)} %momentum_hbm.1) | copy-start | bytes 147460
  0.0 27.6 %copy-start.1 = (f32[2,16,128]{2,1,0:T(8,128)S(1)}, f32[2,16,128]{2,1,0:T(8,128)}, u32[]{:S(2)}) copy-start(f32[2,16,128]{2,1,0:T(8,128)} %density_hbm.1) | copy-start | bytes 49156
  0.0 27.7 %copy-start.2 = (f32[2,16,128]{2,1,0:T(8,128)S(1)}, f32[2,16,128]{2,1,0:T(8,128)}, u32[]{:S(2)}) copy-start(f32[2,16,128]{2,1,0:T(8,128)} %energy_hbm.1) | copy-start | bytes 49156

commit v4 on v3

--- a/solution.py
+++ b/solution.py
@@ -313,6 +313,12 @@
     def other(offset):
         return lax.rem(me + offset, devices)
 
+    barrier = pltpu.get_barrier_semaphore()
+
+    @pl.loop(1, devices)
+    def _(offset):
+        pl.semaphore_signal(barrier, inc=1, device_id=place(other(offset)), device_id_type=mesh_id)
+
     middle = (slice(2, 4), slice(8, 24), slice(None))
     loads = [
         pltpu.make_async_copy(source, target, load_sem.at[number])
@@ -329,12 +335,6 @@
     ]
     for load in loads:
         load.start()
-
-    barrier = pltpu.get_barrier_semaphore()
-
-    @pl.loop(1, devices)
-    def _(offset):
-        pl.semaphore_signal(barrier, inc=1, device_id=place(other(offset)), device_id_type=mesh_id)
 
     @pl.when(gx == 0)
     def _():

time: 29.4 us -> 29.4 us (level)
  no operation moved by 1% of the time
where the time goes in v4:
time: 29.4 us; the launch traced here: 29.2 us
  Pallas kernels  27.6 us (94%)
  other arithmetic  1.54 us (5%)
    pallas_call x1, Pallas kernels, kernel_shards(): pl.pallas_call(functools.partial(step_kernel, nx_dev, ny_dev), out_shape=...  27.6 us
    add x1, other arithmetic, kernel_shards(): return state + change  1.54 us

profile of v4, /device:TPU:0, one launch (start us, length us, event | category | flops | bytes accessed | tf_op | source)
XLA Modules:
  0.0 29.2 jit_solution(10538044364929366027)
XLA Ops:
  0.0 0.0 copy-start
  0.0 0.0 copy-start.1
  0.0 0.0 copy-start.2
  0.0 27.6 %lu_step.1 = f32[5,2,16,128]{3,2,1,0:T(8,128)} custom-call(f32[2,16,128]{2,1,0:T(8,128)} %density_hbm.1, f32[3,2,16,128]{3,2,1,0:T(8,128)} %momentum_hbm.1, f32[2,16,128]{2,1,0:T(8,128)} %energy_hbm.1, f32[5,2,16,128]{3,2,1,0:T(8,128)} %forcing_hbm.1, f32[5,2,5]{2,1,0:T(2,128)} %bitcast.5, f32[5,5]{1,0:T(8,128)} %inverse_hbm.1), custom_call_target="tpu_custom_call" | custom-call | tf_op jit(solution)/shard_map/lu_step/pallas_call | solution.py:577
  27.6 0.0 copy-done
  27.6 0.0 copy-done.1
  27.7 0.0 copy-done.2
  27.7 1.5 %maximum_add_fusion = f32[5,2,16,128]{3,2,1,0:T(8,128)} fusion(f32[5,2,16,128]{3,2,1,0:T(8,128)} %lu_step.1, f32[1,2,16,128]{3,2,1,0:T(8,128)S(1)} %bitcast.4, f32[3,2,16,128]{3,2,1,0:T(8,128)S(1)} %copy-done, f32[1,2,16,128]{3,2,1,0:T(8,128)S(1)} %bitcast.3), kind=kLoop, calls=%fused_computation | loop fusion | flops 61440 | bytes 245760 | tf_op jit(solution)/shard_map/add | solution.py:611
Async XLA Ops:
  0.0 27.6 %copy-start = (f32[3,2,16,128]{3,2,1,0:T(8,128)S(1)}, f32[3,2,16,128]{3,2,1,0:T(8,128)}, u32[]{:S(2)}) copy-start(f32[3,2,16,128]{3,2,1,0:T(8,128)} %momentum_hbm.1) | copy-start | bytes 147460
  0.0 27.6 %copy-start.1 = (f32[2,16,128]{2,1,0:T(8,128)S(1)}, f32[2,16,128]{2,1,0:T(8,128)}, u32[]{:S(2)}) copy-start(f32[2,16,128]{2,1,0:T(8,128)} %density_hbm.1) | copy-start | bytes 49156
  0.0 27.7 %copy-start.2 = (f32[2,16,128]{2,1,0:T(8,128)S(1)}, f32[2,16,128]{2,1,0:T(8,128)}, u32[]{:S(2)}) copy-start(f32[2,16,128]{2,1,0:T(8,128)} %energy_hbm.1) | copy-start | bytes 49156
